TPU v7x, 256 devices: a whole 4x4x8 slice. The times are simulated.
256 devices in a mesh: rep: 8 (over z_lo, core), shard: 32 (over z_hi, y, x).
Axes of the slice: x: 4, y: 4, z: 8 (z_hi: 2, z_lo: 4; z = z_hi * 4 + z_lo), core: 2. Of those that a mesh axis runs over, the one named last changes fastest.
Arguments:
- grad_parts: bfloat16 [8, 32, 128, 5120], P('rep', 'shard'), may hold values from -2 to 2
- momentum: float32 [8, 128, 5120], P('rep', 'shard'), may hold values from -6 to 6
- params: float32 [128, 5120], P('shard'), may hold values from -6 to 6
- indices: int32 [8, 128, 640], P('rep', 'shard'), may hold values from 0 to 63, as said below
Outputs:
- new_momentum: float32 [8, 128, 5120], P('rep', 'shard')
- new_params: float32 [128, 5120], P('shard')
Inputs may be any that keep to these rules, and one draw needn't show every extreme that they name: `indices`: the 8 positions of one block and replica are distinct.
All inputs are finite; a program needn't handle non-finite values.
Results may differ from a plain program's by a relative error of at most 0.0003.
Values sent between devices are 32-bit elements; how exact they have to be, the bound alone decides.
A program may use at most 64 MiB of HBM per device.

v0:
```python
import math

import jax
import jax.numpy as jnp
from jax import lax
from jax.sharding import PartitionSpec as P

SPAN = 64
KEEP = 8


momentum_decay = 0.9
step_size = 1.0


def dct_table():
    freq = lax.iota(jnp.float32, SPAN)[:, None]
    place = lax.iota(jnp.float32, SPAN)[None, :]
    table = jnp.cos(math.pi * (place + 0.5) * freq / SPAN)
    factor = jnp.where(freq == 0.0, math.sqrt(1.0 / SPAN), math.sqrt(2.0 / SPAN))
    return table * factor


def spread(values, picks):
    slots = lax.iota(jnp.int32, SPAN)
    onehot = (picks[..., None] == slots).astype(jnp.float32)
    return jnp.sum(values[..., None] * onehot, axis=-2)


def apply_table(block, table_pair):
    rows_here = block.shape[0]
    flat = block.reshape(-1, 2 * SPAN)
    out = jnp.dot(
        flat, table_pair, precision=lax.Precision.HIGHEST, preferred_element_type=jnp.float32
    )
    return out.reshape(rows_here, -1)


def process(gsum, moment, picks, param_block, forward_pair, inverse_pair):
    rows_here, width = gsum.shape
    blocks = width // SPAN
    blend = momentum_decay * moment + gsum
    coef = apply_table(blend, forward_pair).reshape(rows_here, blocks, SPAN)
    chosen_at = picks.reshape(rows_here, blocks, KEEP)
    chosen = jnp.take_along_axis(coef, chosen_at, axis=2)
    dense = spread(chosen, chosen_at)
    new_moment = blend - apply_table(dense.reshape(rows_here, width), inverse_pair)
    replicas = lax.axis_size("rep")
    all_values, all_places = (
        lax.all_gather(chosen.reshape(1, rows_here, width // 8), "rep", axis=0, tiled=True),
        lax.all_gather(chosen_at.reshape(1, rows_here, width // 8), "rep", axis=0, tiled=True),
    )

    def add_replica(index, total):
        values = all_values[index].reshape(rows_here, blocks, KEEP)
        places = all_places[index].reshape(rows_here, blocks, KEEP)
        return total + spread(values, places)

    total = lax.fori_loop(
        0, replicas, add_replica, jnp.zeros((rows_here, blocks, SPAN), jnp.float32)
    )
    average = (total / replicas).reshape(rows_here, width)
    new_param = param_block - step_size * apply_table(average, inverse_pair)
    return (new_moment, new_param)


def local(grad_parts, momentum, params, indices):
    table = dct_table()
    forward_pair = jnp.kron(jnp.eye(2, dtype=jnp.float32), table.T)
    inverse_pair = jnp.kron(jnp.eye(2, dtype=jnp.float32), table)
    local_grad = grad_parts[0, 0]
    moment = momentum[0]
    picks = indices[0]
    gsum = lax.psum_scatter(
        local_grad.astype(jnp.float32), "shard", scatter_dimension=0, tiled=True
    )
    new_moment, new_params = process(gsum, moment, picks, params, forward_pair, inverse_pair)
    return (new_moment[None], new_params)


def solution(mesh):
    in_specs = (
        P("rep", "shard", None, None),
        P("rep", "shard", None),
        P("shard", None),
        P("rep", "shard", None),
    )
    out_specs = (P("rep", "shard", None), P("shard", None))
    return jax.shard_map(local, mesh=mesh, in_specs=in_specs, out_specs=out_specs, check_vma=False)
```

profile of v0, /device:TPU:1, one launch (start us, length us, event | category | flops | bytes accessed | tf_op | source)
XLA Modules:
  0.0 502.0 jit_solution(14266419027209109067)
XLA Ops:
  7.2 3.1 bitcast_convert_fusion
  10.4 0.6 copy-done
  11.3 0.3 cosine_multiply_fusion
  12.3 0.6 dynamic-slice
  13.5 17.0 %all_gather.6 = s32[8,4,640]{2,1,0:T(4,128)S(1)} all-gather(s32[1,4,640]{2,1,0:T(4,128)S(1)} %copy-done), channel_id=1, replica_groups=mesh['rep'=8,'shard'=32] {'rep'}, dimensions={0}, use_global_device_ids=true | all-gather | bytes 92160 | tf_op jit(solution)/shard_map/all_gather | solution.py:51
  30.5 398.6 %all-reduce.3.cloned.1.call-done = f32[128,5120]{1,0:T(8,128)} async-done(((f32[128,5120]{1,0:T(8,128)}), f32[128,5120]{1,0:T(8,128)}) %all-reduce.3.cloned.1.call-update) | async-done | bytes 2621456
  429.2 1.0 dynamic-slice_add_fusion
  430.2 0.2 fusion.3
  430.5 20.5 %gather_fusion = f32[2560]{0:T(1024)S(1)} fusion(f32[4,80,64]{2,1,0:T(8,128)S(1)} %reshape_reshape.9, s32[2560]{0:T(1024)S(1)} %reshape.198), kind=kCustom, calls=%fused_computation | custom fusion | bytes 51200 | tf_op jit(solution)/shard_map/jit(take_along_axis)/gather | solution.py:45
  451.2 0.2 select_reduce_fusion.1
  451.7 0.2 fusion.4
  451.9 0.7 subtract_bitcast_fusion
  452.6 35.6 %all_gather.7 = f32[8,4,640]{2,1,0:T(4,128)S(1)} all-gather(f32[1,4,640]{2,1,0:T(4,128)S(1)} %and_select_fusion.1), channel_id=1, replica_groups=mesh['rep'=8,'shard'=32] {'rep'}, dimensions={0}, use_global_device_ids=true | all-gather | bytes 92160 | tf_op jit(solution)/shard_map/all_gather | solution.py:50
  488.2 5.8 %while.14 = (s32[]{:T(128)}, f32[4,80,64]{1,2,0:T(8,128)S(1)}, s32[8,4,640]{2,1,0:T(4,128)S(1)}, f32[8,4,640]{2,1,0:T(4,128)S(1)}, s32[]{:T(128)}, /*index=5*/s32[]{:T(128)}) while((s32[]{:T(128)}, f32[4,80,64]{1,2,0:T(8,128)S(1)}, s32[8,4,640]{2,1,0:T(4,128)S(1)}, f32[8,4,640]{2,1,0:T(4,128)S(1)}, s32[]{:T(128)}, ...), condition=%wide.region_4.5_spmd.clone, body=%wide.region_2.4_spmd.clone.sunk | while | flops 512003 | bytes 471135 | solution.py:59
  488.6 0.2 select_reduce_fusion.3
  489.4 0.2 select_reduce_fusion.3
  490.1 0.2 select_reduce_fusion.3
  490.8 0.2 select_reduce_fusion.3
  491.5 0.2 select_reduce_fusion.3
  492.3 0.2 select_reduce_fusion.3
  493.0 0.2 select_reduce_fusion.3
  493.7 0.2 select_reduce_fusion.3
  494.2 0.2 fusion.5
  494.5 0.7 sub.7
  (90 shorter events, 5.5 us)
Async XLA Ops:
  7.2 422.0 %all-reduce.3.cloned.1.call-start = ((), (), s32[]{:S(2)}) async-start(), calls=%async_computation | async-start | bytes 5242880
  10.3 0.7 copy-start
  10.3 2.0 copy-start.3
  10.3 418.8 %copy-start.1 = (f32[1,4,5120]{2,1,0:T(4,128)S(1)}, f32[1,4,5120]{2,1,0:T(4,128)}, u32[]{:S(2)}) copy-start(f32[1,4,5120]{2,1,0:T(4,128)} %param.7) | copy-start | bytes 245764
  488.2 6.3 %copy-start.2 = (f32[4,5120]{1,0:T(4,128)S(1)}, f32[4,5120]{1,0:T(4,128)}, u32[]{:S(2)}) copy-start(f32[4,5120]{1,0:T(4,128)} %param.8) | copy-start | bytes 245764
Sparse Core Ops, SparseCore 0:
  10.6 418.4 all-reduce.2
where the time goes:
time: 502 us
  waiting for transfers between devices  399 us (79%)
  blocking collectives  52.6 us (10%)
  local copies, waits for them, and re-layouts  26.6 us (5%)
  between operations  14.9 us (3%)
  other arithmetic  8.16 us (2%)
    unnamed x2, waiting for transfers between devices  399 us
    all_gather x1, blocking collectives, process(): lax.all_gather(chosen.reshape(1, rows_here, width // 8), 'rep', axis=0, t...  35.6 us
    gather x4, local copies, waits for them, and re-layouts, process(): chosen = jnp.take_along_axis(coef, chosen_at, axis=2)  20.7 us
    all_gather x1, blocking collectives, process(): lax.all_gather(chosen_at.reshape(1, rows_here, width // 8), 'rep', axis=0...  17 us
  transfers between devices with their start and end apart: 1, of which 1 were waited for; matrix products, arithmetic and copies ran while one was open for 0% of the time, Pallas kernels for 0%

commit v1 on v0

v1 whole, which is shorter than its diff:
```python
import functools
import math

import jax
import jax.numpy as jnp
import numpy as np
from jax import lax
from jax.experimental import pallas as pl
from jax.experimental.pallas import tpu as pltpu
from jax.sharding import PartitionSpec as P

SPAN = 64
KEEP = 8
REPS = 8
DECAY = 0.9
LANES = 128
TILES = 8
ROWS4 = 4
BLOCK = TILES * ROWS4
WIDE = TILES * LANES
LAST = 4
CHUNKS = 5
MESH = pl.DeviceIdType.MESH
F32 = jnp.float32


def tables():
    freq = np.arange(SPAN, dtype=np.float64)[:, None]
    place = np.arange(SPAN, dtype=np.float64)[None, :]
    table = np.cos(math.pi * (place + 0.5) * freq / SPAN)
    table = table * np.where(freq == 0.0, math.sqrt(1.0 / SPAN), math.sqrt(2.0 / SPAN))
    pair = np.kron(np.eye(2), table)
    return pair.T.astype(np.float32), pair.astype(np.float32)


def dot(a, b):
    return jnp.dot(a, b, precision=lax.Precision.HIGHEST, preferred_element_type=F32)


def lookup(values, lanes):
    return jnp.take_along_axis(values, lanes, axis=1, mode="promise_in_bounds")


def kernel(
    g_hbm, m_hbm, p_hbm, i_hbm, f_hbm, b_hbm, nm_hbm, np_hbm,
    gb, m_v, p_v, i_v, f_v, b_v, nm_v, np_v, relay,
    stage, zout, rz_last, rf, rd, rs, rf_l, rd_l, rs_l,
    s1, r2, s2, rz, s1_l, r2_l, coef, blend, picks, slots, kept,
    in_sem, out_sem, p1_send, p1_recv, p2_send, p2_recv, z_send, z_recv,
    i_send, i_recv, c_send, c_recv, l_send, l_recv,
):
    rep, shard = lax.axis_index("rep"), lax.axis_index("shard")
    zlo, core = rep // 2, rep % 2
    zhi, y, x = shard // 16, (shard // 4) % 4, shard % 4

    def at(zhi_, y_, x_):
        return (rep, zhi_ * 16 + y_ * 4 + x_)

    def step_x(d):
        return at(zhi, y, (x + d) % 4)

    def step_y(d):
        return at(zhi, (y + d) % 4, x)

    z_partner = at(1 - zhi, y, x)
    core_partner = (zlo * 2 + 1 - core, shard)

    def step_l(d):
        return (((zlo + d) % 4) * 2 + core, shard)

    def swap(c):
        return (core + c) % 2

    def first(c, d):
        s = swap(c)
        return at(zhi, (y + s * d) % 4, (x + (1 - s) * d) % 4)

    def second(c, d):
        s = swap(c)
        return at(zhi, (y + (1 - s) * d) % 4, (x + s * d) % 4)

    def place_a(c):
        return x + swap(c) * (y - x)

    def place_b(c):
        return y + swap(c) * (x - y)

    def remote(src, dst, send, recv, device):
        return pltpu.make_async_remote_copy(
            src_ref=src, dst_ref=dst, send_sem=send, recv_sem=recv,
            device_id=device, device_id_type=MESH,
        )

    sent = []

    def go(copy):
        copy.start()
        sent.append(copy)

    def cols(c):
        return pl.ds(c * WIDE, WIDE)

    loads = {}
    for n, c in enumerate((0, LAST, 1, 2, 3)):
        loads[c] = pltpu.make_async_copy(g_hbm.at[:, cols(c)], gb.at[c], in_sem.at[c])
        loads[c].start()
    small = [
        pltpu.make_async_copy(i_hbm, i_v, in_sem.at[5]),
        pltpu.make_async_copy(m_hbm, m_v, in_sem.at[6]),
        pltpu.make_async_copy(p_hbm, p_v, in_sem.at[7]),
        pltpu.make_async_copy(f_hbm, f_v, in_sem.at[8]),
        pltpu.make_async_copy(b_hbm, b_v, in_sem.at[9]),
    ]
    for copy in small:
        copy.start()

    barrier = pltpu.get_barrier_semaphore()
    peers = [step_x(1), step_x(-1 + 4), step_y(1), step_y(-1 + 4), step_x(2), step_y(2)]
    peers += [z_partner, core_partner] + [step_l(d) for d in (1, 2, 3)]
    for peer in peers:
        pl.semaphore_signal(barrier, inc=1, device_id=peer, device_id_type=MESH)

    upper = lax.broadcasted_iota(jnp.int32, (8, LANES), 0) // 4
    lane = lax.broadcasted_iota(jnp.int32, (8, LANES), 1)
    low_half = upper == 0

    def convert(c):
        loads[c].wait()
        s = swap(c)

        def group(k, carry):
            z_, y_ = k // 4, k % 4
            rows = pl.ds(pl.multiple_of(k * 16, 16), 16)
            for t in range(0, TILES, 2):
                one = gb[c, rows, t * LANES:(t + 1) * LANES].astype(F32)
                two = gb[c, rows, (t + 1) * LANES:(t + 2) * LANES].astype(F32)
                for h in range(2):
                    u, v = one[8 * h:8 * h + 8], two[8 * h:8 * h + 8]
                    for q in range(2):
                        x_ = 2 * h + q
                        if q == 0:
                            piece = jnp.where(low_half, u, pltpu.roll(v, 4, 0))
                        else:
                            piece = jnp.where(low_half, pltpu.roll(u, 4, 0), v)
                        a_, b_ = x_ + s * (y_ - x_), y_ + s * (x_ - y_)
                        stage[c, a_, z_, b_, 4 * t:4 * t + 8, :] = piece
            return carry

        lax.fori_loop(0, 8, group, 0)

    def half(c, q, h):
        if c == LAST:
            return zout.at[q, pl.ds(2 * h, 2)]
        return stage.at[c, q, h]

    def got(c, kind, h):
        if c == LAST:
            return (rf_l, rd_l, rs_l)[kind].at[h]
        return (rf, rd, rs)[kind].at[c, h]

    def p1_copy(c, n, q, h, kind, slot, d):
        return remote(
            half(c, q, h), got(c, kind, slot), p1_send.at[c, n], p1_recv.at[c, n], first(c, d)
        )

    def p1_start(c):
        p = place_a(c)
        up, down, far = (p + 1) % 4, (p + 3) % 4, (p + 2) % 4
        go(p1_copy(c, 0, far, 0, 0, 0, 1))
        go(p1_copy(c, 1, far, 1, 0, 1, 3))
        go(p1_copy(c, 2, up, 1, 1, 1, 1))
        go(p1_copy(c, 3, down, 0, 1, 0, 3))

    def p1_wait(c, n, kind, slot):
        p = place_a(c)
        p1_copy(c, n, p, slot, kind, slot, 1).wait_recv()

    def p1_sum(c):
        p = place_a(c)
        up, down = (p + 1) % 4, (p + 3) % 4
        p1_wait(c, 0, 0, 0)
        half(c, up, 0)[...] += got(c, 0, 0)[...]
        go(p1_copy(c, 4, up, 0, 2, 0, 1))
        p1_wait(c, 1, 0, 1)
        half(c, down, 1)[...] += got(c, 0, 1)[...]
        go(p1_copy(c, 5, down, 1, 2, 1, 3))

    def p2_block(c, q):
        return s1_l.at[q] if c == LAST else s1.at[c, q]

    def p2_got(c, d):
        return r2_l.at[d - 1] if c == LAST else r2.at[c, d - 1]

    def p2_copy(c, q, d):
        return remote(
            p2_block(c, q), p2_got(c, d), p2_send.at[c, d - 1], p2_recv.at[c, d - 1], second(c, d)
        )

    def p1_end(c):
        p = place_a(c)
        p1_wait(c, 3, 1, 0)
        p1_wait(c, 2, 1, 1)
        p1_wait(c, 4, 2, 0)
        p1_wait(c, 5, 2, 1)
        for h in range(2):
            own, direct, summed = half(c, p, h), got(c, 1, h), got(c, 2, h)
            if c == LAST:
                for n in range(2):
                    s1_l[2 * h + n] = own[n] + direct[n] + summed[n]
            else:
                for n in range(4):
                    s1[c, n, h] = own[n] + direct[n] + summed[n]
        q = place_b(c)
        for d in (2, 1, 3):
            go(p2_copy(c, (q + d) % 4, d))

    def z_copy(c):
        return remote(s2.at[c, 1 - zhi], rz.at[c], z_send.at[c], z_recv.at[c], z_partner)

    def p2_end(c):
        q = place_b(c)
        for d in (1, 3, 2):
            p2_copy(c, q, d).wait_recv()
        if c == LAST:
            return s1_l[q] + r2_l[0] + r2_l[1] + r2_l[2]
        s2[c] = s1[c, q] + r2[c, 0] + r2[c, 1] + r2[c, 2]
        go(z_copy(c))

    def zl_copy():
        return remote(zout, rz_last, z_send.at[LAST], z_recv.at[LAST], z_partner)

    def zl_start():
        for a_ in range(4):
            zout[a_] = stage[LAST, a_, 1 - zhi]
        zl_copy().start()

    def zl_end():
        zl_copy().wait()
        for a_ in range(4):
            zout[a_] = stage[LAST, a_, zhi] + rz_last[a_]

    def pair(buf, c):
        return buf.at[c, pl.ds(zlo * 2, 2)]

    def i_core():
        return remote(picks.at[rep], picks.at[rep], i_send.at[0], i_recv.at[0], core_partner)

    def i_pair(d):
        both = picks.at[pl.ds(zlo * 2, 2)]
        return remote(both, both, i_send.at[d], i_recv.at[d], step_l(d))

    def i_start():
        small[0].wait()
        for c in range(CHUNKS):
            four = i_v[:, c * LANES:(c + 1) * LANES]
            picks[rep, c, 0:4, :] = four
            picks[rep, c, 4:8, :] = four
        go(i_core())

    def i_forward():
        i_core().wait_recv()
        for d in (2, 1, 3):
            go(i_pair(d))

    def i_end():
        for d in (1, 2, 3):
            i_pair(d).wait_recv()

    def make_slots(c):
        nothing = 16 - 16 * upper
        base = 16 * upper + 8 * (lane // SPAN)
        want = lane % SPAN

        def one(r, carry):
            have = picks[r, c]
            for v in range(4):
                found = nothing
                for j in range(KEEP):
                    source = base + (32 * v + j)
                    found = jnp.where(lookup(have, source) == want, source, found)
                slots[r, c, v] = found
            return carry

        lax.fori_loop(0, REPS, one, 0)

    def c_core(c):
        return remote(kept.at[c, rep], kept.at[c, rep], c_send.at[c], c_recv.at[c], core_partner)

    def c_pair(c, d):
        both = pair(kept, c)
        return remote(both, both, l_send.at[c, d - 1], l_recv.at[c, d - 1], step_l(d))

    def to_rows(ref, c):
        for t in range(TILES):
            at_ = (c * TILES + t) * LANES
            relay[0, 4 * t:4 * t + 4, :] = ref[:, at_:at_ + LANES]
        return relay[0]

    def from_rows(value, ref, c, n):
        relay[n] = value
        for t in range(TILES):
            at_ = (c * TILES + t) * LANES
            ref[:, at_:at_ + LANES] = relay[n, 4 * t:4 * t + 4, :]

    def transform(c, grad):
        now = DECAY * to_rows(m_v, c) + grad
        blend[c] = now
        out = dot(now, f_v[...])
        coef[c] = out
        places = picks[rep, c] + SPAN * ((lane // KEEP) % 2)
        got_ = jnp.zeros((8, LANES), F32)
        for v in range(4):
            mine = lane // 16 == 2 * v + upper
            got_ = jnp.where(mine, lookup(out[8 * v:8 * v + 8], places), got_)
        kept[c, rep] = got_
        go(c_core(c))

    def z_end(c):
        z_copy(c).wait_recv()
        transform(c, s2[c, zhi] + rz[c])

    def c_forward(c):
        c_core(c).wait_recv()
        for d in (2, 1, 3):
            go(c_pair(c, d))

    outs = []

    def put(ref, hbm, c, n):
        copy = pltpu.make_async_copy(ref.at[:, cols(c)], hbm.at[:, cols(c)], out_sem.at[n, c])
        copy.start()
        outs.append(copy)

    def momentum_out(c):
        mine = kept[c, rep]
        dense = jnp.concatenate([lookup(mine, slots[rep, c, v]) for v in range(4)], axis=0)
        from_rows(blend[c] - dot(dense, b_v[...]), nm_v, c, 1)
        put(nm_v, nm_hbm, c, 0)

    def params_out(c):
        for d in (1, 2, 3):
            c_pair(c, d).wait_recv()
        parts = []
        for v in range(4):
            total = lookup(kept[c, 0], slots[0, c, v])
            for r in range(1, REPS):
                total = total + lookup(kept[c, r], slots[r, c, v])
            parts.append(total)
        average = jnp.concatenate(parts, axis=0) / REPS
        from_rows(to_rows(p_v, c) - dot(average, b_v[...]), np_v, c, 2)
        put(np_v, np_hbm, c, 1)

    convert(0)
    pl.semaphore_wait(barrier, len(peers))
    p1_start(0)
    convert(LAST)
    zl_start()
    convert(1)
    p1_start(1)
    i_start()
    p1_sum(0)
    convert(2)
    p1_start(2)
    i_forward()
    p1_end(0)
    p1_sum(1)
    convert(3)
    p1_start(3)
    for copy in small[1:]:
        copy.wait()
    i_end()
    make_slots(0)
    p2_end(0)
    p1_end(1)
    p1_sum(2)
    make_slots(1)
    zl_end()
    p1_start(LAST)
    p2_end(1)
    make_slots(2)
    p1_end(2)
    p1_sum(3)
    z_end(0)
    make_slots(3)
    make_slots(4)
    p2_end(2)
    p1_sum(LAST)
    c_forward(0)
    momentum_out(0)
    p1_end(3)
    z_end(1)
    p1_end(LAST)
    c_forward(1)
    p2_end(3)
    momentum_out(1)
    z_end(2)
    grad_last = p2_end(LAST)
    transform(LAST, grad_last)
    c_forward(2)
    params_out(0)
    c_forward(LAST)
    z_end(3)
    params_out(1)
    c_forward(3)
    momentum_out(2)
    momentum_out(LAST)
    momentum_out(3)
    params_out(2)
    params_out(LAST)
    params_out(3)
    for copy in sent:
        copy.wait_send()
    for copy in outs:
        copy.wait()


def local(grad_parts, momentum, params, indices):
    forward, back = tables()
    any_ = pl.BlockSpec(memory_space=pl.ANY)
    vmem = pltpu.VMEM
    dma = pltpu.SemaphoreType.DMA
    n = CHUNKS - 1
    block = (BLOCK, LANES)
    new_momentum, new_params = pl.pallas_call(
        kernel,
        out_shape=(
            jax.ShapeDtypeStruct(momentum.shape[1:], F32),
            jax.ShapeDtypeStruct(params.shape, F32),
        ),
        in_specs=[any_] * 6,
        out_specs=(any_, any_),
        scratch_shapes=[
            vmem((CHUNKS, 128, WIDE), jnp.bfloat16),
            vmem(params.shape, F32),
            vmem(params.shape, F32),
            vmem(indices.shape[1:], jnp.int32),
            vmem((LANES, LANES), F32),
            vmem((LANES, LANES), F32),
            vmem(params.shape, F32),
            vmem(params.shape, F32),
            vmem((3, *block), F32),
            vmem((CHUNKS, 4, 2, 4, *block), F32),
            vmem((4, 4, *block), F32),
            vmem((4, 4, *block), F32),
            vmem((n, 2, 4, *block), F32),
            vmem((n, 2, 4, *block), F32),
            vmem((n, 2, 4, *block), F32),
            vmem((2, 2, *block), F32),
            vmem((2, 2, *block), F32),
            vmem((2, 2, *block), F32),
            vmem((n, 4, 2, *block), F32),
            vmem((n, 3, 2, *block), F32),
            vmem((n, 2, *block), F32),
            vmem((n, *block), F32),
            vmem((4, *block), F32),
            vmem((3, *block), F32),
            vmem((CHUNKS, *block), F32),
            vmem((CHUNKS, *block), F32),
            vmem((REPS, CHUNKS, 8, LANES), jnp.int32),
            vmem((REPS, CHUNKS, 4, 8, LANES), jnp.int32),
            vmem((CHUNKS, REPS, 8, LANES), F32),
            dma((10,)),
            dma((2, CHUNKS)),
            dma((CHUNKS, 6)),
            dma((CHUNKS, 6)),
            dma((CHUNKS, 3)),
            dma((CHUNKS, 3)),
            dma((CHUNKS,)),
            dma((CHUNKS,)),
            dma((4,)),
            dma((4,)),
            dma((CHUNKS,)),
            dma((CHUNKS,)),
            dma((CHUNKS, 3)),
            dma((CHUNKS, 3)),
        ],
        compiler_params=pltpu.CompilerParams(
            collective_id=0, has_side_effects=True, vmem_limit_bytes=40 << 20
        ),
        name="step",
    )(grad_parts[0, 0], momentum[0], params, indices[0], forward, back)
    return new_momentum[None], new_params


def solution(mesh):
    in_specs = (
        P("rep", "shard", None, None),
        P("rep", "shard", None),
        P("shard", None),
        P("rep", "shard", None),
    )
    out_specs = (P("rep", "shard", None), P("shard", None))
    return jax.shard_map(local, mesh=mesh, in_specs=in_specs, out_specs=out_specs, check_vma=False)
```

time: 502 us -> 60.7 us (0.12)
  waiting for transfers between devices: 399 us -> 0 us
  Pallas kernels: 0 us -> 53 us
  blocking collectives: 52.6 us -> 0 us
  local copies, waits for them, and re-layouts: 26.6 us -> 6.73 us
  between operations: 14.9 us -> 0.65 us
  other arithmetic: 8.16 us -> 0 us
    unnamed x2 -> x0, waiting for transfers between devices: 399 us -> none
    pallas_call x0 -> x1, Pallas kernels: none -> 53 us  [local(): pl.pallas_call(kernel, out_shape=(jax.ShapeDtypeStruct(momentum.shape[1:]...]
    all_gather x2 -> x0, blocking collectives: 52.6 us -> none  [the longest x1 35.6 us: process(): lax.all_gather(chosen.reshape(1, rows_here, width // 8), 'rep', axis=0, t...]
    gather x4 -> x0, local copies, waits for them, and re-layouts: 20.7 us -> none  [process(): chosen = jnp.take_along_axis(coef, chosen_at, axis=2)]
    unnamed x9 -> x14, local copies, waits for them, and re-layouts: 1.25 us -> 6.73 us
  transfers between devices with their start and end apart: 1 -> 0, of which waited for: 1 -> 0; matrix products, arithmetic and copies ran while one was open for 0% -> 0% of each run, Pallas kernels for 0% -> 0%
where the time goes in v1:
time: 60.7 us; the launch traced here: 60.4 us
  Pallas kernels  53 us (87%)
  local copies, waits for them, and re-layouts  6.73 us (11%)
  between operations  0.65 us (1%)
    pallas_call x1, Pallas kernels, local(): pl.pallas_call(kernel, out_shape=(jax.ShapeDtypeStruct(momentum.shape[1:]...  53 us
    unnamed x14, local copies, waits for them, and re-layouts  6.73 us

profile of v1, /device:TPU:1, one launch (start us, length us, event | category | flops | bytes accessed | tf_op | source)
XLA Modules:
  0.0 60.4 jit_solution(14114235929346828713)
XLA Ops:
  0.6 0.0 copy-start
  0.6 1.3 %copy-done = bf16[1,1,128,5120]{3,2,1,0:T(8,128)(2,1)S(1)} copy-done((bf16[1,1,128,5120]{3,2,1,0:T(8,128)(2,1)S(1)}, bf16[1,1,128,5120]{3,2,1,0:T(8,128)(2,1)}, u32[]{:S(2)}) %copy-start) | copy-done | bytes 1310744
  1.9 0.0 copy-start.1
  1.9 0.9 %copy-done.1 = f32[1,4,5120]{2,1,0:T(4,128)S(1)} copy-done((f32[1,4,5120]{2,1,0:T(4,128)S(1)}, f32[1,4,5120]{2,1,0:T(4,128)}, u32[]{:S(2)}) %copy-start.1) | copy-done | bytes 81944
  2.8 0.0 copy-start.2
  2.8 0.9 %copy-done.2 = f32[4,5120]{1,0:T(4,128)S(1)} copy-done((f32[4,5120]{1,0:T(4,128)S(1)}, f32[4,5120]{1,0:T(4,128)}, u32[]{:S(2)}) %copy-start.2) | copy-done | bytes 81944
  3.7 0.0 copy-start.3
  3.7 0.8 %copy-done.3 = f32[128,128]{1,0:T(8,128)S(1)} copy-done((f32[128,128]{1,0:T(8,128)S(1)}, f32[128,128]{1,0:T(8,128)}, u32[]{:S(2)}) %copy-start.3) | copy-done | bytes 65560
  4.6 0.0 copy-start.4
  4.6 0.8 %copy-done.4 = f32[128,128]{1,0:T(8,128)S(1)} copy-done((f32[128,128]{1,0:T(8,128)S(1)}, f32[128,128]{1,0:T(8,128)}, u32[]{:S(2)}) %copy-start.4) | copy-done | bytes 65560
  5.4 0.0 copy-start.5
  5.4 0.7 %copy-done.5 = s32[1,4,640]{2,1,0:T(4,128)S(1)} copy-done((s32[1,4,640]{2,1,0:T(4,128)S(1)}, s32[1,4,640]{2,1,0:T(4,128)}, u32[]{:S(2)}) %copy-start.5) | copy-done | bytes 10264
  6.1 53.0 %step.1 = (f32[4,5120]{1,0:T(4,128)S(1)}, f32[4,5120]{1,0:T(4,128)S(1)}) custom-call(bf16[128,5120]{1,0:T(8,128)(2,1)S(1)} %bitcast.4, f32[4,5120]{1,0:T(4,128)S(1)} %bitcast.5, f32[4,5120]{1,0:T(4,128)S(1)} %copy-done.2, s32[4,640]{1,0:T(4,128)S(1)} %bitcast.7, f32[128,128]{1,0:T(8,128)S(1)} %copy-done.4, f32[128,128]{1,0:T(8,128)S(1)} %copy-done.3), custom_call_target="tpu_custom_call" | custom-call | tf_op jit(solution)/shard_map/step/pallas_call | solution.py:424
  59.1 0.6 %copy.10 = f32[1,4,5120]{2,1,0:T(4,128)} copy(f32[1,4,5120]{2,1,0:T(4,128)S(1)} %bitcast.6) | data formatting | bytes 163840
  59.8 0.6 %copy.11 = f32[4,5120]{1,0:T(4,128)} copy(f32[4,5120]{1,0:T(4,128)S(1)} %get-tuple-element.9) | data formatting | bytes 163840
Async XLA Ops:
  0.6 1.3 %copy-start = (bf16[1,1,128,5120]{3,2,1,0:T(8,128)(2,1)S(1)}, bf16[1,1,128,5120]{3,2,1,0:T(8,128)(2,1)}, u32[]{:S(2)}) copy-start(bf16[1,1,128,5120]{3,2,1,0:T(8,128)(2,1)} %param.6) | copy-start | bytes 3932164
  1.9 0.9 %copy-start.1 = (f32[1,4,5120]{2,1,0:T(4,128)S(1)}, f32[1,4,5120]{2,1,0:T(4,128)}, u32[]{:S(2)}) copy-start(f32[1,4,5120]{2,1,0:T(4,128)} %param.7) | copy-start | bytes 245764
  2.8 0.9 %copy-start.2 = (f32[4,5120]{1,0:T(4,128)S(1)}, f32[4,5120]{1,0:T(4,128)}, u32[]{:S(2)}) copy-start(f32[4,5120]{1,0:T(4,128)} %p_hbm.1) | copy-start | bytes 245764
  3.7 0.8 %copy-start.3 = (f32[128,128]{1,0:T(8,128)S(1)}, f32[128,128]{1,0:T(8,128)}, u32[]{:S(2)}) copy-start(f32[128,128]{1,0:T(8,128)} %constant.5.clone.b_hbm) | copy-start | bytes 196612
  4.6 0.8 %copy-start.4 = (f32[128,128]{1,0:T(8,128)S(1)}, f32[128,128]{1,0:T(8,128)}, u32[]{:S(2)}) copy-start(f32[128,128]{1,0:T(8,128)} %constant.4.clone.f_hbm) | copy-start | bytes 196612
  5.4 0.7 %copy-start.5 = (s32[1,4,640]{2,1,0:T(4,128)S(1)}, s32[1,4,640]{2,1,0:T(4,128)}, u32[]{:S(2)}) copy-start(s32[1,4,640]{2,1,0:T(4,128)} %param.9) | copy-start | bytes 30724

commit v2 on v0

v2 whole, which is shorter than its diff:
```python
import functools
import math

import jax
import jax.numpy as jnp
import numpy as np
from jax import lax
from jax.experimental import pallas as pl
from jax.experimental.pallas import tpu as pltpu
from jax.sharding import PartitionSpec as P

SPAN = 64
KEEP = 8
REPS = 8
DECAY = 0.9
LANES = 128
TILES = 8
BLOCK = 4 * TILES
WIDE = TILES * LANES
CHUNKS = ((0, 2, 0), (2, 2, 1), (4, 1, 0))
INDEX_TILES = 5
MESH = pl.DeviceIdType.MESH
F32 = jnp.float32


def tables():
    freq = np.arange(SPAN, dtype=np.float64)[:, None]
    place = np.arange(SPAN, dtype=np.float64)[None, :]
    table = np.cos(math.pi * (place + 0.5) * freq / SPAN)
    table = table * np.where(freq == 0.0, math.sqrt(1.0 / SPAN), math.sqrt(2.0 / SPAN))
    pair = np.kron(np.eye(2), table)
    return pair.T.astype(np.float32), pair.astype(np.float32)


def dot(a, b):
    return jnp.dot(a, b, precision=lax.Precision.HIGHEST, preferred_element_type=F32)


def lookup(values, lanes):
    return jnp.take_along_axis(values, lanes, axis=1, mode="promise_in_bounds")


def kernel(names, *refs):
    r_ = dict(zip(names, refs))
    rep, shard = lax.axis_index("rep"), lax.axis_index("shard")
    zlo, core = rep // 2, rep % 2
    zhi, y, x = shard // 16, (shard // 4) % 4, shard % 4

    def at(zhi_, y_, x_):
        return (rep, zhi_ * 16 + y_ * 4 + x_)

    def step_x(d):
        return at(zhi, y, (x + d) % 4)

    def step_y(d):
        return at(zhi, (y + d) % 4, x)

    core_partner = (zlo * 2 + 1 - core, shard)

    def step_l(d, far=0):
        half_ = zhi + far * (1 - 2 * zhi)
        return (((zlo + d) % 4) * 2 + core, half_ * 16 + y * 4 + x)

    def swap(c):
        return (core + CHUNKS[c][2]) % 2

    def first(c, d):
        s = swap(c)
        return at(zhi, (y + s * d) % 4, (x + (1 - s) * d) % 4)

    def second(c, d):
        s = swap(c)
        return at(zhi, (y + (1 - s) * d) % 4, (x + s * d) % 4)

    def place_a(c):
        return x + swap(c) * (y - x)

    def place_b(c):
        return y + swap(c) * (x - y)

    def buf(name, c):
        return r_[name + str(c)]

    def sems(name, c, n):
        return r_[name + "_send"].at[c, n], r_[name + "_recv"].at[c, n]

    def remote(src, dst, pair, device):
        return pltpu.make_async_remote_copy(
            src_ref=src, dst_ref=dst, send_sem=pair[0], recv_sem=pair[1],
            device_id=device, device_id_type=MESH,
        )

    sent = []

    def go(copy):
        copy.start()
        sent.append(copy)

    def flush():
        while sent:
            sent.pop(0).wait_send()

    loads = []
    for c, (tile, count, _) in enumerate(CHUNKS):
        loads.append(
            pltpu.make_async_copy(
                r_["g_hbm"].at[:, pl.ds(tile * WIDE, count * WIDE)], buf("gb", c), r_["in_sem"].at[c]
            )
        )
    small = [
        pltpu.make_async_copy(r_[a], r_[b], r_["in_sem"].at[len(CHUNKS) + n])
        for n, (a, b) in enumerate(
            (("i_hbm", "i_v"), ("m_hbm", "m_v"), ("p_hbm", "p_v"), ("f_hbm", "f_v"), ("b_hbm", "b_v"))
        )
    ]
    for copy in loads[:1] + small[:1] + loads[1:] + small[1:]:
        copy.start()

    barrier = pltpu.get_barrier_semaphore()
    peers = [step_x(1), step_x(3), step_y(1), step_y(3), step_x(2), step_y(2)]
    peers += [core_partner] + [step_l(d) for d in (1, 2, 3)] + [step_l(d, 1) for d in range(4)]
    for peer in peers:
        pl.semaphore_signal(barrier, inc=1, device_id=peer, device_id_type=MESH)

    upper = lax.broadcasted_iota(jnp.int32, (8, LANES), 0) // 4
    lane = lax.broadcasted_iota(jnp.int32, (8, LANES), 1)
    low_half = upper == 0

    def convert(c, z_):
        s = swap(c)
        gb, stage = buf("gb", c), buf("stage", c)

        def group(y_, carry):
            rows = pl.ds(pl.multiple_of(z_ * 64 + y_ * 16, 16), 16)
            for t in range(0, CHUNKS[c][1] * TILES, 2):
                one = gb[rows, t * LANES:(t + 1) * LANES].astype(F32)
                two = gb[rows, (t + 1) * LANES:(t + 2) * LANES].astype(F32)
                for h in range(2):
                    u, v = one[8 * h:8 * h + 8], two[8 * h:8 * h + 8]
                    for q in range(2):
                        x_ = 2 * h + q
                        if q == 0:
                            piece = jnp.where(low_half, u, pltpu.roll(v, 4, 0))
                        else:
                            piece = jnp.where(low_half, pltpu.roll(u, 4, 0), v)
                        a_, b_ = x_ + s * (y_ - x_), y_ + s * (x_ - y_)
                        stage[a_, z_, b_, 4 * t:4 * t + 8, :] = piece
            return carry

        lax.fori_loop(0, 4, group, 0)

    def half(c, q, h):
        return buf("stage", c).at[q, h]

    def got(c, kind, h):
        return buf(("rf", "rd", "rs")[kind], c).at[h]

    def p1_copy(c, n, q, h, kind, slot, d):
        return remote(half(c, q, h), got(c, kind, slot), sems("p1", c, n), first(c, d))

    def p1_forward(c):
        far = (place_a(c) + 2) % 4
        go(p1_copy(c, 0, far, 0, 0, 0, 1))
        go(p1_copy(c, 1, far, 1, 0, 1, 3))

    def p1_direct(c):
        p = place_a(c)
        go(p1_copy(c, 2, (p + 1) % 4, 1, 1, 1, 1))
        go(p1_copy(c, 3, (p + 3) % 4, 0, 1, 0, 3))

    def p1_wait(c, n, kind, slot):
        p1_copy(c, n, place_a(c), slot, kind, slot, 1).wait_recv()

    def p1_sum(c):
        p = place_a(c)
        up, down = (p + 1) % 4, (p + 3) % 4
        p1_wait(c, 0, 0, 0)
        half(c, up, 0)[...] += got(c, 0, 0)[...]
        go(p1_copy(c, 4, up, 0, 2, 0, 1))
        p1_wait(c, 1, 0, 1)
        half(c, down, 1)[...] += got(c, 0, 1)[...]
        go(p1_copy(c, 5, down, 1, 2, 1, 3))

    def p2_copy(c, q, d):
        return remote(buf("s1", c).at[q], buf("r2", c).at[d - 1], sems("p2", c, d - 1), second(c, d))

    def p1_end(c):
        p, s1 = place_a(c), buf("s1", c)
        for n, kind, slot in ((3, 1, 0), (2, 1, 1), (4, 2, 0), (5, 2, 1)):
            p1_wait(c, n, kind, slot)
        for h in range(2):
            own, direct, summed = half(c, p, h), got(c, 1, h), got(c, 2, h)
            for n in range(4):
                s1[n, h] = own[n] + direct[n] + summed[n]
        q = place_b(c)
        for d in (2, 1, 3):
            go(p2_copy(c, (q + d) % 4, d))

    def z_copy(c):
        return remote(buf("s2", c).at[1 - zhi], buf("rz", c), sems("z", c, 0), step_l(0, 1))

    def p2_end(c):
        q, r2 = place_b(c), buf("r2", c)
        for d in (1, 3, 2):
            p2_copy(c, q, d).wait_recv()
        buf("s2", c)[...] = buf("s1", c)[q] + r2[0] + r2[1] + r2[2]

    def pick_copy(d):
        mine = r_["picks"].at[core, zlo]
        return remote(mine, mine, sems("pick", 0, d), step_l(d))

    def pick_far():
        return remote(r_["picks"].at[core, zlo], r_["far_picks"], sems("pick", 0, 4), step_l(0, 1))

    def core_copy(ref, name, n):
        return remote(ref.at[core], ref.at[core], sems(name, 0, n), core_partner)

    def kept_copy(c, d, far):
        source = r_["far_kept"].at[c] if far else r_["kept"].at[0, zlo, c]
        n = 3 + d if far else d - 1
        return remote(source, r_["kept"].at[far, zlo, c], sems("kept", c, n), step_l(d, far))

    ways = ((0, 1), (2, 0), (1, 1), (3, 1), (1, 0), (3, 0), (2, 1))

    def kept_end(c):
        for d, far in ways:
            kept_copy(c, d, far).wait_recv()

    picks, slots, spots, kept, kept_sum = r_["picks"], r_["slots"], r_["spots"], r_["kept"], r_["kept_sum"]

    def i_start():
        small[0].wait()
        for t in range(INDEX_TILES):
            picks[core, zlo, t] = r_["i_v"][:, t * LANES:(t + 1) * LANES]
        for d in (2, 1, 3):
            go(pick_copy(d))
        go(pick_far())

    def i_middle():
        for d in (1, 3, 2):
            pick_copy(d).wait_recv()
        go(core_copy(picks, "pick", 0))
        pick_far().wait_recv()

    def doubled(four):
        return jnp.concatenate([four, pltpu.roll(four, LANES - 16, 1)], axis=0)

    def make_slots():
        rows = INDEX_TILES * REPS * 8
        for t in range(INDEX_TILES):
            for r in range(REPS):
                at_ = (t * REPS + r) * 8
                spots[at_:at_ + 8, :] = doubled(picks[r // 4, r % 4, t]).astype(F32)
        from_row = lax.broadcasted_iota(jnp.int32, (LANES, 2 * LANES), 0)
        column = lax.broadcasted_iota(jnp.int32, (LANES, 2 * LANES), 1)
        to_lane = column % LANES
        wide = lax.broadcasted_iota(jnp.int32, (rows, LANES), 1)
        want = (wide % SPAN).astype(F32)
        tile_of = lax.broadcasted_iota(jnp.int32, (rows, LANES), 0) // (REPS * 8)
        base = KEEP * (wide // SPAN) + 16 * (tile_of % 2)
        have = spots[...].astype(jnp.bfloat16)

        def one(v, carry):
            found = jnp.full((rows, LANES), -1, jnp.int32)
            for j in range(0, KEEP, 2):
                source = 32 * v + KEEP * (to_lane // SPAN) + j + column // LANES
                pick = (from_row == source).astype(F32).astype(jnp.bfloat16)
                spread = jnp.dot(have, pick, preferred_element_type=F32)
                for k in range(2):
                    here = spread[:, k * LANES:(k + 1) * LANES] == want
                    found = jnp.where(here, base + (32 * v + j + k), found)
            slots[v] = found
            return carry

        lax.fori_loop(0, 4, one, 0)

    def slot(v, t, core_, z_):
        at_ = (t * REPS + core_ * 4 + z_) * 8
        return slots[v, pl.ds(pl.multiple_of(at_, 8), 8), :]

    def spread(values, where):
        return jnp.where(where >= 0, lookup(values, jnp.maximum(where, 0)), 0.0)

    def to_rows(ref, out):
        for t in range(INDEX_TILES * TILES):
            out[4 * t:4 * t + 4, :] = ref[:, t * LANES:(t + 1) * LANES]

    def from_rows(value, relay, ref, c):
        tile, count = CHUNKS[c][:2]
        relay[0:count * BLOCK, :] = value
        for t in range(count * TILES):
            at_ = (tile * TILES + t) * LANES
            ref[:, at_:at_ + LANES] = relay[4 * t:4 * t + 4, :]

    def rows_of(c):
        tile, count = CHUNKS[c][:2]
        return slice(tile * BLOCK, (tile + count) * BLOCK)

    def choose(out, positions, c):
        found = jnp.zeros((8, LANES), F32)
        for t in range(CHUNKS[c][1]):
            places = doubled(positions[t])
            if t % 2:
                places = pltpu.roll(places, 16, 1)
            places = places + SPAN * ((lane // KEEP) % 2)
            for v in range(4):
                mine = lane // 16 == 2 * v + t % 2
                part = out[t * BLOCK + 8 * v:t * BLOCK + 8 * v + 8]
                found = jnp.where(mine, lookup(part, places), found)
        return found

    def transform(c):
        tile, count = CHUNKS[c][:2]
        s2 = buf("s2", c)
        own = DECAY * r_["m_rows"][rows_of(c), :] + s2[zhi]
        r_["blend"][rows_of(c), :] = own
        out = dot(jnp.concatenate([own, s2[1 - zhi]], axis=0), r_["f_v"][...])
        rows = count * BLOCK
        kept[0, zlo, c] = choose(out[:rows], [picks[core, zlo, tile + t] for t in range(count)], c)
        r_["far_kept"][c] = choose(out[rows:], [r_["far_picks"][tile + t] for t in range(count)], c)
        for d, far in ways:
            go(kept_copy(c, d, far))
        go(z_copy(c))

    def momentum_out(c):
        tile, count = CHUNKS[c][:2]
        z_copy(c).wait_recv()
        now = r_["blend"][rows_of(c), :] + buf("rz", c)[...]
        own = [slot(v, t, core, zlo) for t in range(tile, tile + count) for v in range(4)]
        dense = jnp.where(jnp.concatenate(own, axis=0) >= 0, dot(now, r_["f_v"][...]), 0.0)
        from_rows(now - dot(dense, r_["b_v"][...]), r_["relay0"], r_["nm_out"], c)

    def core_sum(core_):
        parts = []
        for t in range(INDEX_TILES):
            for v in range(4):
                total = spread(kept_sum[core_, 0, t // 2], slot(v, t, core_, 0))
                for z_ in range(1, 4):
                    total = total + spread(kept_sum[core_, z_, t // 2], slot(v, t, core_, z_))
                parts.append(total)
        return jnp.concatenate(parts, axis=0)

    def params_out():
        for c in range(len(CHUNKS)):
            kept_end(c)
        kept_sum[core] = kept[0] + kept[1]
        copy = core_copy(kept_sum, "pick", 5)
        go(copy)
        r_["relay1"][...] = core_sum(core)
        momentum_out(2)
        copy.wait_recv()
        average = (r_["relay1"][...] + core_sum(1 - core)) / REPS
        r_["relay1"][...] = r_["p_rows"][...] - dot(average, r_["b_v"][...])
        for t in range(INDEX_TILES * TILES):
            r_["np_out"][:, t * LANES:(t + 1) * LANES] = r_["relay1"][4 * t:4 * t + 4, :]

    loads[0].wait()
    convert(0, 0)
    convert(0, 1)
    pl.semaphore_wait(barrier, len(peers))
    p1_forward(0)
    p1_direct(0)
    loads[1].wait()
    convert(1, 0)
    convert(1, 1)
    p1_forward(1)
    i_start()
    loads[2].wait()
    convert(2, 0)
    convert(2, 1)
    p1_sum(0)
    p1_direct(1)
    p1_forward(2)
    for copy in small[1:]:
        copy.wait()
    to_rows(r_["m_v"], r_["m_rows"])
    to_rows(r_["p_v"], r_["p_rows"])
    p1_sum(1)
    p1_direct(2)
    i_middle()
    p1_end(0)
    p1_sum(2)
    p1_end(1)
    p2_end(0)
    transform(0)
    p1_end(2)
    p2_end(1)
    transform(1)
    p2_end(2)
    transform(2)
    core_copy(picks, "pick", 0).wait_recv()
    make_slots()
    flush()
    momentum_out(0)
    momentum_out(1)
    params_out()
    flush()


def scratches(shape):
    vmem, dma = pltpu.VMEM, pltpu.SemaphoreType.DMA
    made = {
        "m_v": vmem(shape, F32),
        "p_v": vmem(shape, F32),
        "i_v": vmem((4, INDEX_TILES * LANES), jnp.int32),
        "f_v": vmem((LANES, LANES), F32),
        "b_v": vmem((LANES, LANES), F32),
        "m_rows": vmem((INDEX_TILES * BLOCK, LANES), F32),
        "p_rows": vmem((INDEX_TILES * BLOCK, LANES), F32),
        "blend": vmem((INDEX_TILES * BLOCK, LANES), F32),
        "relay0": vmem((INDEX_TILES * BLOCK, LANES), F32),
        "relay1": vmem((INDEX_TILES * BLOCK, LANES), F32),
        "picks": vmem((2, 4, INDEX_TILES, 4, LANES), jnp.int32),
        "slots": vmem((4, INDEX_TILES * REPS * 8, LANES), jnp.int32),
        "kept": vmem((2, 4, len(CHUNKS), 8, LANES), F32),
        "kept_sum": vmem((2, 4, len(CHUNKS), 8, LANES), F32),
        "far_kept": vmem((len(CHUNKS), 8, LANES), F32),
        "far_picks": vmem((INDEX_TILES, 4, LANES), jnp.int32),
        "spots": vmem((INDEX_TILES * REPS * 8, LANES), F32),
    }
    for c, (_, count, _) in enumerate(CHUNKS):
        block = (count * BLOCK, LANES)
        made["gb" + str(c)] = vmem((128, count * WIDE), jnp.bfloat16)
        made["stage" + str(c)] = vmem((4, 2, 4, *block), F32)
        for name in ("rf", "rd", "rs"):
            made[name + str(c)] = vmem((2, 4, *block), F32)
        made["s1" + str(c)] = vmem((4, 2, *block), F32)
        made["r2" + str(c)] = vmem((3, 2, *block), F32)
        made["s2" + str(c)] = vmem((2, *block), F32)
        made["rz" + str(c)] = vmem(block, F32)
    made["in_sem"] = dma((len(CHUNKS) + 5,))
    for name, count in (("p1", 6), ("p2", 3), ("z", 1), ("pick", 6), ("kept", 7)):
        for end in ("_send", "_recv"):
            made[name + end] = dma((len(CHUNKS), count))
    return made


def local(grad_parts, momentum, params, indices):
    forward, back = tables()
    hbm = pl.BlockSpec(memory_space=pltpu.HBM)
    vmem = pl.BlockSpec(memory_space=pltpu.VMEM)
    made = scratches(params.shape)
    names = ("g_hbm", "m_hbm", "p_hbm", "i_hbm", "f_hbm", "b_hbm", "nm_out", "np_out", *made)
    operands = (grad_parts[0, 0], momentum[0], params, indices[0], jnp.asarray(forward), jnp.asarray(back))
    new_momentum, new_params = pl.pallas_call(
        functools.partial(kernel, names),
        out_shape=(pltpu.VMEM(params.shape, F32),) * 2,
        in_specs=[hbm] * 6,
        out_specs=(vmem, vmem),
        scratch_shapes=list(made.values()),
        compiler_params=pltpu.CompilerParams(
            collective_id=0, has_side_effects=True, vmem_limit_bytes=60 << 20
        ),
        name="step",
    )(*(pltpu.with_memory_space_constraint(v, pltpu.HBM) for v in operands))
    return new_momentum[None], new_params


def solution(mesh):
    in_specs = (
        P("rep", "shard", None, None),
        P("rep", "shard", None),
        P("shard", None),
        P("rep", "shard", None),
    )
    out_specs = (P("rep", "shard", None), P("shard", None))
    return jax.shard_map(local, mesh=mesh, in_specs=in_specs, out_specs=out_specs, check_vma=False)
```

time: 502 us -> 40.2 us (0.08)
  waiting for transfers between devices: 399 us -> 0 us
  blocking collectives: 52.6 us -> 0 us
  Pallas kernels: 0 us -> 38.2 us
  local copies, waits for them, and re-layouts: 26.6 us -> 1.27 us
  between operations: 14.9 us -> 0.64 us
  other arithmetic: 8.16 us -> 0 us
    unnamed x2 -> x0, waiting for transfers between devices: 399 us -> none
    all_gather x2 -> x0, blocking collectives: 52.6 us -> none  [the longest x1 35.6 us: process(): lax.all_gather(chosen.reshape(1, rows_here, width // 8), 'rep', axis=0, t...]
    pallas_call x0 -> x1, Pallas kernels: none -> 38.2 us  [local(): pl.pallas_call(functools.partial(kernel, names), out_shape=(pltpu.VMEM(pa...]
    gather x4 -> x0, local copies, waits for them, and re-layouts: 20.7 us -> none  [process(): chosen = jnp.take_along_axis(coef, chosen_at, axis=2)]
  transfers between devices with their start and end apart: 1 -> 0, of which waited for: 1 -> 0; matrix products, arithmetic and copies ran while one was open for 0% -> 0% of each run, Pallas kernels for 0% -> 0%
where the time goes in v2:
time: 40.2 us; the launch traced here: 40.1 us
  Pallas kernels  38.2 us (95%)
  local copies, waits for them, and re-layouts  1.27 us (3%)
  between operations  0.64 us (2%)
    pallas_call x1, Pallas kernels, local(): pl.pallas_call(functools.partial(kernel, names), out_shape=(pltpu.VMEM(pa...  38.2 us
    unnamed x2, local copies, waits for them, and re-layouts  1.27 us

profile of v2, /device:TPU:1, one launch (start us, length us, event | category | flops | bytes accessed | tf_op | source)
XLA Modules:
  0.0 40.1 jit_solution(4847592050449596177)
XLA Ops:
  0.6 38.2 %step.1 = (f32[4,5120]{1,0:T(4,128)S(1)}, f32[4,5120]{1,0:T(4,128)S(1)}) custom-call(bf16[128,5120]{1,0:T(8,128)(2,1)} %bitcast.5, f32[4,5120]{1,0:T(4,128)} %bitcast.6, f32[4,5120]{1,0:T(4,128)} %refs_2_.1, s32[4,640]{1,0:T(4,128)} %bitcast.7, f32[128,128]{1,0:T(8,128)} %constant.4.clone.refs_4_, f32[128,128]{1,0:T(8,128)} %constant.5.clone.refs_5_), custom_call_target="tpu_custom_call" | custom-call | tf_op jit(solution)/shard_map/step/pallas_call | solution.py:445
  38.9 0.6 %copy.10 = f32[1,4,5120]{2,1,0:T(4,128)} copy(f32[1,4,5120]{2,1,0:T(4,128)S(1)} %bitcast.4) | data formatting | bytes 163840
  39.5 0.6 %copy.11 = f32[4,5120]{1,0:T(4,128)} copy(f32[4,5120]{1,0:T(4,128)S(1)} %get-tuple-element.7) | data formatting | bytes 163840

commit v3 on v2

--- a/solution.py
+++ b/solution.py
@@ -96,9 +96,10 @@
         copy.start()
         sent.append(copy)
 
-    def flush():
-        while sent:
-            sent.pop(0).wait_send()
+    def flush(count=None):
+        for copy in sent[:count]:
+            copy.wait_send()
+        del sent[:count]
 
     loads = []
     for c, (tile, count, _) in enumerate(CHUNKS):
@@ -320,7 +321,6 @@
         r_["far_kept"][c] = choose(out[rows:], [r_["far_picks"][tile + t] for t in range(count)], c)
         for d, far in ways:
             go(kept_copy(c, d, far))
-        go(z_copy(c))
 
     def momentum_out(c):
         tile, count = CHUNKS[c][:2]
@@ -330,29 +330,35 @@
         dense = jnp.where(jnp.concatenate(own, axis=0) >= 0, dot(now, r_["f_v"][...]), 0.0)
         from_rows(now - dot(dense, r_["b_v"][...]), r_["relay0"], r_["nm_out"], c)
 
-    def core_sum(core_):
+    def core_sum(core_, c):
+        tile, count = CHUNKS[c][:2]
         parts = []
-        for t in range(INDEX_TILES):
+        for t in range(tile, tile + count):
             for v in range(4):
-                total = spread(kept_sum[core_, 0, t // 2], slot(v, t, core_, 0))
+                total = spread(kept_sum[c, core_, 0], slot(v, t, core_, 0))
                 for z_ in range(1, 4):
-                    total = total + spread(kept_sum[core_, z_, t // 2], slot(v, t, core_, z_))
+                    total = total + spread(kept_sum[c, core_, z_], slot(v, t, core_, z_))
                 parts.append(total)
         return jnp.concatenate(parts, axis=0)
 
-    def params_out():
-        for c in range(len(CHUNKS)):
-            kept_end(c)
-        kept_sum[core] = kept[0] + kept[1]
-        copy = core_copy(kept_sum, "pick", 5)
-        go(copy)
-        r_["relay1"][...] = core_sum(core)
-        momentum_out(2)
-        copy.wait_recv()
-        average = (r_["relay1"][...] + core_sum(1 - core)) / REPS
-        r_["relay1"][...] = r_["p_rows"][...] - dot(average, r_["b_v"][...])
-        for t in range(INDEX_TILES * TILES):
-            r_["np_out"][:, t * LANES:(t + 1) * LANES] = r_["relay1"][4 * t:4 * t + 4, :]
+    def kept_swap(c):
+        mine = kept_sum.at[c, core]
+        return remote(mine, mine, sems("swap", c, 0), core_partner)
+
+    def kept_add(c):
+        kept_end(c)
+        kept_sum[c, core] = kept[0, :, c] + kept[1, :, c]
+        go(kept_swap(c))
+
+    def params_own(c):
+        r_["relay1"][rows_of(c), :] = core_sum(core, c)
+
+    def params_out(c):
+        tile, count = CHUNKS[c][:2]
+        kept_swap(c).wait_recv()
+        average = (r_["relay1"][rows_of(c), :] + core_sum(1 - core, c)) / REPS
+        result = r_["p_rows"][rows_of(c), :] - dot(average, r_["b_v"][...])
+        from_rows(result, r_["relay2"], r_["np_out"], c)
 
     loads[0].wait()
     convert(0, 0)
@@ -381,19 +387,32 @@
     p1_end(0)
     p1_sum(2)
     p1_end(1)
+    p1_end(2)
+    early = len(sent)
     p2_end(0)
     transform(0)
-    p1_end(2)
+    go(z_copy(0))
     p2_end(1)
     transform(1)
+    go(z_copy(1))
     p2_end(2)
     transform(2)
+    go(z_copy(2))
     core_copy(picks, "pick", 0).wait_recv()
     make_slots()
-    flush()
+    flush(early)
+    kept_add(0)
+    params_own(0)
     momentum_out(0)
+    kept_add(1)
+    params_own(1)
+    params_out(0)
     momentum_out(1)
-    params_out()
+    kept_add(2)
+    params_own(2)
+    params_out(1)
+    momentum_out(2)
+    params_out(2)
     flush()
 
 
@@ -409,11 +428,12 @@
         "p_rows": vmem((INDEX_TILES * BLOCK, LANES), F32),
         "blend": vmem((INDEX_TILES * BLOCK, LANES), F32),
         "relay0": vmem((INDEX_TILES * BLOCK, LANES), F32),
+        "relay2": vmem((INDEX_TILES * BLOCK, LANES), F32),
         "relay1": vmem((INDEX_TILES * BLOCK, LANES), F32),
         "picks": vmem((2, 4, INDEX_TILES, 4, LANES), jnp.int32),
         "slots": vmem((4, INDEX_TILES * REPS * 8, LANES), jnp.int32),
         "kept": vmem((2, 4, len(CHUNKS), 8, LANES), F32),
-        "kept_sum": vmem((2, 4, len(CHUNKS), 8, LANES), F32),
+        "kept_sum": vmem((len(CHUNKS), 2, 4, 8, LANES), F32),
         "far_kept": vmem((len(CHUNKS), 8, LANES), F32),
         "far_picks": vmem((INDEX_TILES, 4, LANES), jnp.int32),
         "spots": vmem((INDEX_TILES * REPS * 8, LANES), F32),
@@ -429,10 +449,35 @@
         made["s2" + str(c)] = vmem((2, *block), F32)
         made["rz" + str(c)] = vmem(block, F32)
     made["in_sem"] = dma((len(CHUNKS) + 5,))
-    for name, count in (("p1", 6), ("p2", 3), ("z", 1), ("pick", 6), ("kept", 7)):
+    for name, count in (("p1", 6), ("p2", 3), ("z", 1), ("pick", 5), ("kept", 7), ("swap", 1)):
         for end in ("_send", "_recv"):
             made[name + end] = dma((len(CHUNKS), count))
     return made
+
+
+def write(a_ref, b_ref, a_out, b_out, sem):
+    copies = [
+        pltpu.make_async_copy(a_ref, a_out.at[0], sem.at[0]),
+        pltpu.make_async_copy(b_ref, b_out, sem.at[1]),
+    ]
+    for copy in copies:
+        copy.start()
+    for copy in copies:
+        copy.wait()
+
+
+def write_out(new_momentum, new_params):
+    vmem, hbm = pl.BlockSpec(memory_space=pltpu.VMEM), pl.BlockSpec(memory_space=pltpu.HBM)
+    shape = new_params.shape
+    return pl.pallas_call(
+        write,
+        out_shape=(pltpu.HBM((1, *shape), F32), pltpu.HBM(shape, F32)),
+        in_specs=[vmem, vmem],
+        out_specs=(hbm, hbm),
+        scratch_shapes=[pltpu.SemaphoreType.DMA((2,))],
+        compiler_params=pltpu.CompilerParams(vmem_limit_bytes=1 << 20),
+        name="write",
+    )(new_momentum, new_params)
 
 
 def local(grad_parts, momentum, params, indices):
@@ -453,7 +498,7 @@
         ),
         name="step",
     )(*(pltpu.with_memory_space_constraint(v, pltpu.HBM) for v in operands))
-    return new_momentum[None], new_params
+    return write_out(new_momentum, new_params)
 
 
 def solution(mesh):

time: 40.2 us -> 39.4 us (0.980)
  local copies, waits for them, and re-layouts: 1.27 us -> 0 us
    unnamed x2 -> x0, local copies, waits for them, and re-layouts: 1.27 us -> none
    pallas_call x0 -> x1, Pallas kernels: none -> 0.68 us  [write_out(): pl.pallas_call(write, out_shape=(pltpu.HBM((1, *shape), F32), pltpu.HBM(s...]
where the time goes in v3:
time: 39.4 us; the launch traced here: 39.3 us
  Pallas kernels  38.6 us (98%)
  between operations  0.64 us (2%)
    pallas_call x1, Pallas kernels, local(): pl.pallas_call(functools.partial(kernel, names), out_shape=(pltpu.VMEM(pa...  37.9 us

profile of v3, /device:TPU:1, one launch (start us, length us, event | category | flops | bytes accessed | tf_op | source)
XLA Modules:
  0.0 39.3 jit_solution(16636605428713835946)
XLA Ops:
  0.6 37.9 %step.1 = (f32[4,5120]{1,0:T(4,128)S(1)}, f32[4,5120]{1,0:T(4,128)S(1)}) custom-call(bf16[128,5120]{1,0:T(8,128)(2,1)} %bitcast.3, f32[4,5120]{1,0:T(4,128)} %bitcast.4, f32[4,5120]{1,0:T(4,128)} %refs_2_.1, s32[4,640]{1,0:T(4,128)} %bitcast.5, f32[128,128]{1,0:T(8,128)} %constant.4.clone.refs_4_, f32[128,128]{1,0:T(8,128)} %constant.5.clone.refs_5_), custom_call_target="tpu_custom_call" | custom-call | tf_op jit(solution)/shard_map/step/pallas_call | solution.py:490
  38.6 0.7 %write.1 = (f32[1,4,5120]{2,1,0:T(4,128)}, f32[4,5120]{1,0:T(4,128)}) custom-call(f32[4,5120]{1,0:T(4,128)S(1)} %get-tuple-element.4.a_ref, f32[4,5120]{1,0:T(4,128)S(1)} %get-tuple-element.5.b_ref), custom_call_target="tpu_custom_call" | custom-call | tf_op jit(solution)/shard_map/write/pallas_call | solution.py:472

commit v4 on v3

--- a/solution.py
+++ b/solution.py
@@ -17,7 +17,7 @@
 TILES = 8
 BLOCK = 4 * TILES
 WIDE = TILES * LANES
-CHUNKS = ((0, 2, 0), (2, 2, 1), (4, 1, 0))
+CHUNKS = ((4, 1, 0), (0, 2, 1), (2, 2, 0))
 INDEX_TILES = 5
 MESH = pl.DeviceIdType.MESH
 F32 = jnp.float32
@@ -100,6 +100,12 @@
         for copy in sent[:count]:
             copy.wait_send()
         del sent[:count]
+
+    barrier = pltpu.get_barrier_semaphore()
+    peers = [step_x(1), step_x(3), step_y(1), step_y(3), step_x(2), step_y(2)]
+    peers += [core_partner] + [step_l(d) for d in (1, 2, 3)] + [step_l(d, 1) for d in range(4)]
+    for peer in peers:
+        pl.semaphore_signal(barrier, inc=1, device_id=peer, device_id_type=MESH)
 
     loads = []
     for c, (tile, count, _) in enumerate(CHUNKS):
@@ -116,12 +122,6 @@
     ]
     for copy in loads[:1] + small[:1] + loads[1:] + small[1:]:
         copy.start()
-
-    barrier = pltpu.get_barrier_semaphore()
-    peers = [step_x(1), step_x(3), step_y(1), step_y(3), step_x(2), step_y(2)]
-    peers += [core_partner] + [step_l(d) for d in (1, 2, 3)] + [step_l(d, 1) for d in range(4)]
-    for peer in peers:
-        pl.semaphore_signal(barrier, inc=1, device_id=peer, device_id_type=MESH)
 
     upper = lax.broadcasted_iota(jnp.int32, (8, LANES), 0) // 4
     lane = lax.broadcasted_iota(jnp.int32, (8, LANES), 1)

time: 39.4 us -> 38.7 us (0.982)
  Pallas kernels: 38.6 us -> 37.9 us
    pallas_call x1, Pallas kernels: 37.9 us -> 37.2 us  [local(): pl.pallas_call(functools.partial(kernel, names), out_shape=(pltpu.VMEM(pa...]
where the time goes in v4:
time: 38.7 us; the launch traced here: 38.5 us
  Pallas kernels  37.9 us (98%)
  between operations  0.64 us (2%)
    pallas_call x1, Pallas kernels, local(): pl.pallas_call(functools.partial(kernel, names), out_shape=(pltpu.VMEM(pa...  37.2 us

profile of v4, /device:TPU:1, one launch (start us, length us, event | category | flops | bytes accessed | tf_op | source)
XLA Modules:
  0.0 38.5 jit_solution(5456798197088767622)
XLA Ops:
  0.6 37.2 %step.1 = (f32[4,5120]{1,0:T(4,128)S(1)}, f32[4,5120]{1,0:T(4,128)S(1)}) custom-call(bf16[128,5120]{1,0:T(8,128)(2,1)} %bitcast.3, f32[4,5120]{1,0:T(4,128)} %bitcast.4, f32[4,5120]{1,0:T(4,128)} %refs_2_.1, s32[4,640]{1,0:T(4,128)} %bitcast.5, f32[128,128]{1,0:T(8,128)} %constant.4.clone.refs_4_, f32[128,128]{1,0:T(8,128)} %constant.5.clone.refs_5_), custom_call_target="tpu_custom_call" | custom-call | tf_op jit(solution)/shard_map/step/pallas_call | solution.py:490
  37.8 0.7 %write.1 = (f32[1,4,5120]{2,1,0:T(4,128)}, f32[4,5120]{1,0:T(4,128)}) custom-call(f32[4,5120]{1,0:T(4,128)S(1)} %get-tuple-element.4.a_ref, f32[4,5120]{1,0:T(4,128)S(1)} %get-tuple-element.5.b_ref), custom_call_target="tpu_custom_call" | custom-call | tf_op jit(solution)/shard_map/write/pallas_call | solution.py:472
